TPU v7x, 32 devices: a whole 2x2x4 slice. The times are simulated.
32 devices in a mesh: grp: 2 (over y), row: 8 (over z, x), layer: 2 (over core).
Axes of the slice: x: 2, y: 2, z: 4, core: 2. Of those that a mesh axis runs over, the one named last changes fastest.
Arguments:
- train_codes: bfloat16 [8192, 2, 4096], P(('grp', 'row'), 'layer'), parts along dimension 0, may hold values from -4 to 4
- block_scales: float32 [8192, 2, 32], P(('grp', 'row'), 'layer'), parts along dimension 0, may hold values from 0.0004 to 0.004
- queries: bfloat16 [512, 2, 4096], P('row', 'layer'), may hold values from -6 to 6
- left_factor: float32 [2, 64, 64], P('layer'), may hold values from -1 to 5, as said below
- right_factor: float32 [2, 64, 64], P('layer'), may hold values from -1 to 5, as said below
Outputs:
- influence: float32 [8192, 512], P(('grp', 'row', 'layer')), parts along dimension 0
There are 2 independent parts, one for each index of `grp`. A program takes and returns all parts, laid end to end along the dimension named above; an argument that names none is the same for every part. Nothing has to cross between parts.
Inputs may be any that keep to these rules, and one draw needn't show every extreme that they name: `left_factor`: symmetric. `right_factor`: symmetric.
All inputs are finite; a program needn't handle non-finite values.
Results may differ from a plain program's by a relative error of at most 0.004.
Values may be sent and summed in bfloat16 or wider, within the bound.
A program may use at most 64 MiB of HBM per device.

v0:
```python
import jax
import jax.numpy as jnp
from jax import lax
from jax.sharding import PartitionSpec as P


def precondition(flat, left_factor, right_factor):
    count = flat.shape[0]
    layers = left_factor.shape[0]
    outer = left_factor.shape[1]
    inner = right_factor.shape[1]
    blocks = flat.reshape(count, layers, outer, inner).astype(jnp.float32)
    result = jnp.einsum(
        "lab,nlbc,lcd->nlad", left_factor, blocks, right_factor, precision=lax.Precision.HIGHEST
    )
    return result.astype(jnp.bfloat16).reshape(count, layers * outer * inner)


def per_device(train_codes, block_scales, queries, left_factor, right_factor):
    rows, layers, width = train_codes.shape
    blocks = block_scales.shape[2]
    values = (
        train_codes.reshape(rows, layers, blocks, width // blocks).astype(jnp.float32)
        * block_scales[..., None]
    )
    dequant = values.astype(jnp.bfloat16).reshape(rows, layers * width)
    flat = queries.reshape(queries.shape[0], layers * width)
    sending = precondition(flat, left_factor, right_factor)
    partial_scores = jnp.einsum(
        "rk,qk->rq",
        dequant,
        lax.all_gather(sending, "row", axis=0, tiled=True),
        preferred_element_type=jnp.float32,
    )
    return lax.psum_scatter(partial_scores, "layer", scatter_dimension=0, tiled=True)


def solution(mesh):
    return jax.shard_map(
        per_device,
        mesh=mesh,
        in_specs=(
            P(("grp", "row"), "layer", None),
            P(("grp", "row"), "layer", None),
            P("row", "layer", None),
            P("layer", None, None),
            P("layer", None, None),
        ),
        out_specs=P(("grp", "row", "layer"), None),
        check_vma=False,
    )
```

profile of v0, /device:TPU:0, one launch (start us, length us, event | category | flops | bytes accessed | tf_op | source)
XLA Modules:
  0.0 112.7 jit_solution(14851264782338752870)
XLA Ops:
  6.5 0.0 copy-start
  6.5 0.0 copy-start.4
  6.5 0.0 all-gather.2.cloned.1.call-start
  6.5 2.1 %reshape.35 = bf16[64,64,64]{2,1,0:T(8,128)(2,1)S(1)} reshape(bf16[64,1,4096]{2,0,1:T(8,128)(2,1)} %param.7) | data formatting | bytes 1048576 | tf_op jit(solution)/shard_map/reshape.1
  8.6 0.0 copy-done
  8.6 0.0 copy-start.3
  8.6 1.0 fusion.5
  9.6 0.0 copy-done.4
  9.6 1.8 %convolution_convert_fusion = bf16[64,64,64]{2,1,0:T(8,128)(2,1)S(1)} fusion(f32[64,64,64]{1,2,0:T(8,128)S(1)} %fusion.5, f32[1,64,64]{2,1,0:T(8,128)S(1)} %copy-done.4), kind=kOutput, calls=%fused_computation.4 | convolution fusion | flops 201588736 | bytes 1589248 | tf_op jit(solution)/shard_map/lab,nlbc,lcd->nlad/dot_general | solution.py:13
  11.4 1.6 %reshape.38 = bf16[64,4096]{1,0:T(8,128)(2,1)} reshape(bf16[64,64,64]{2,1,0:T(8,128)(2,1)S(1)} %convolution_convert_fusion) | data formatting | bytes 1048576 | tf_op jit(solution)/shard_map/reshape | solution.py:16
  13.0 0.0 all-gather.2.cloned.1.call-update
  13.1 0.0 reduce-scatter.2.cloned.1.call-start
  13.1 0.0 copy-done.3
  13.1 0.1 copy.6
  13.3 76.1 %all-gather.2.cloned.1.call-done = bf16[512,4096]{1,0:T(8,128)(2,1)} async-done(((bf16[64,4096]{1,0:T(8,128)(2,1)}), bf16[512,4096]{1,0:T(8,128)(2,1)}) %all-gather.2.cloned.1.call-update) | async-done | bytes 4194320 | tf_op jit(solution)/shard_map/all_gather | solution.py:32
  89.3 0.0 copy-start.1
  89.3 0.0 copy-start.2
  89.3 2.3 %mul.16 = f32[512,32,128]{2,1,0:T(8,128)S(1)} broadcast(f32[512,32]{1,0:T(8,128)S(1)} %copy.6), dimensions={0,1} | broadcast | bytes 8454144 | tf_op jit(solution)/shard_map/mul | solution.py:23
  91.6 0.0 copy-done.1
  91.6 1.2 %copy-done.2 = bf16[512,4096]{1,0:T(8,128)(2,1)S(1)} copy-done((bf16[512,4096]{1,0:T(8,128)(2,1)S(1)}, bf16[512,4096]{1,0:T(8,128)(2,1)}, u32[]{:S(2)}) %copy-start.2) | copy-done | bytes 4194328
  92.8 6.1 %fusion.1 = f32[512,512]{1,0:T(8,128)} fusion(bf16[512,4096]{1,0:T(8,128)(2,1)S(1)} %copy-done.2, f32[64,8,32,128]{3,2,1,0:T(8,128)S(1)} %bitcast.26, bf16[512,1,4096]{2,0,1:T(8,128)(2,1)S(1)} %copy-done.1), kind=kOutput, calls=%fused_computation.2 | convolution fusion | flops 2153775104 | bytes 17825792 | tf_op jit(solution)/shard_map/rk,qk->rq/dot_general | solution.py:29
  98.9 0.0 reduce-scatter.2.cloned.1.call-update
  98.9 7.0 %reduce-scatter.2.cloned.1.call-done = f32[256,512]{1,0:T(8,128)} async-done(((f32[512,512]{1,0:T(8,128)}), f32[256,512]{1,0:T(8,128)}) %reduce-scatter.2.cloned.1.call-update) | async-done | bytes 524304 | tf_op jit(solution)/shard_map/reduce_scatter | solution.py:35
Async XLA Ops:
  6.5 2.1 %copy-start = (f32[1,64,64]{2,1,0:T(8,128)S(1)}, f32[1,64,64]{2,1,0:T(8,128)}, u32[]{:S(2)}) copy-start(f32[1,64,64]{2,1,0:T(8,128)} %param.8) | copy-start | bytes 49156
  6.5 3.1 %copy-start.4 = (f32[1,64,64]{2,1,0:T(8,128)S(1)}, f32[1,64,64]{2,1,0:T(8,128)}, u32[]{:S(2)}) copy-start(f32[1,64,64]{2,1,0:T(8,128)} %param.9) | copy-start | bytes 49156
  6.5 82.8 %all-gather.2.cloned.1.call-start = ((), (), s32[]{:S(2)}) async-start(), calls=%async_computation.1 | async-start | bytes 4718592 | tf_op jit(solution)/shard_map/all_gather | solution.py:32
  8.6 4.5 %copy-start.3 = (f32[512,1,32]{0,2,1:T(8,128)S(1)}, f32[512,1,32]{0,2,1:T(8,128)}, u32[]{:S(2)}) copy-start(f32[512,1,32]{0,2,1:T(8,128)} %param.6) | copy-start | bytes 196612
  13.1 92.8 %reduce-scatter.2.cloned.1.call-start = ((), (), s32[]{:S(2)}) async-start(), calls=%async_computation.2 | async-start | bytes 1572864 | tf_op jit(solution)/shard_map/reduce_scatter | solution.py:35
  89.3 2.3 %copy-start.1 = (bf16[512,1,4096]{2,0,1:T(8,128)(2,1)S(1)}, bf16[512,1,4096]{2,0,1:T(8,128)(2,1)}, u32[]{:S(2)}) copy-start(bf16[512,1,4096]{2,0,1:T(8,128)(2,1)} %param.5) | copy-start | bytes 12582916
  89.3 3.5 %copy-start.2 = (bf16[512,4096]{1,0:T(8,128)(2,1)S(1)}, bf16[512,4096]{1,0:T(8,128)(2,1)}, u32[]{:S(2)}) copy-start(bf16[512,4096]{1,0:T(8,128)(2,1)} %all-gather.2.cloned.1.call-done) | copy-start | bytes 12582916
Sparse Core Ops, SparseCore 0:
  13.2 76.0 all-gather.1
  99.0 6.7 reduce-scatter.1
where the time goes:
time: 113 us
  waiting for transfers between devices  83 us (73%)
  between operations  13.5 us (12%)
  matrix products  8.84 us (8%)
  local copies, waits for them, and re-layouts  7.27 us (6%)
    all_gather x1, waiting for transfers between devices, per_device(): lax.all_gather(sending, 'row', axis=0, tiled=True)  76.1 us
    reduce_scatter x1, waiting for transfers between devices, per_device(): lax.psum_scatter(partial_scores, 'layer', scatter_dimension=0, tiled=True)  6.95 us
    dot_general x1, matrix products, per_device(): jnp.einsum('rk,qk->rq', dequant, lax.all_gather(sending, 'row', axis=0, t...  6.09 us
    dot_general x2, matrix products, precondition(): jnp.einsum('lab,nlbc,lcd->nlad', left_factor, blocks, right_factor, preci...  2.76 us
    mul x2, local copies, waits for them, and re-layouts, per_device(): train_codes.reshape(rows, layers, blocks, width // blocks)  2.41 us
  transfers between devices with their start and end apart: 2, of which 2 were waited for; matrix products, arithmetic and copies ran while one was open for 0% of the time, Pallas kernels for 0%

commit v1 on v0

--- a/solution.py
+++ b/solution.py
@@ -1,8 +1,298 @@
+import functools
+
 import jax
 import jax.numpy as jnp
 from jax import lax
+from jax.experimental import pallas as pl
+from jax.experimental.pallas import tpu as pltpu
 from jax.sharding import PartitionSpec as P
 
+MESH = pl.DeviceIdType.MESH
+PLANES = 4
+CHUNKS = 4
+EVENTS = (PLANES - 1) * CHUNKS
+
+
+def split(value):
+    high = value.astype(jnp.bfloat16)
+    return high, (value - high.astype(jnp.float32)).astype(jnp.bfloat16)
+
+
+def dot(a, b):
+    return jnp.dot(a, b, preferred_element_type=jnp.float32)
+
+
+def score_kernel(
+    codes_hbm, scales_ref, queries_ref, left_ref, right_ref, out_ref,
+    codes, train, scales, prepared, spread, mixed, left_diag, right_diag, mine, theirs,
+    codes_sem, recv_sem, up_sem, down_sem, x_sem, y_sem, part_sem, part_recv_sem,
+):
+    rows, width = codes.shape
+    order = left_ref.shape[0]
+    count = queries_ref.shape[0]
+    step = count // CHUNKS
+    half = rows // 2
+    y, at, layer = lax.axis_index("grp"), lax.axis_index("row"), lax.axis_index("layer")
+    z, x = at // 2, at % 2
+    middle = (z * (PLANES - 1 - z)) // 2
+    sign = 1 - 2 * (z // 2)
+    above = {"row": at + 2}
+    below = {"row": at - 2}
+    beside = {"row": at + 1 - 2 * x}
+    across = {"grp": 1 - y}
+    core = {"layer": 1 - layer}
+
+    barrier = pltpu.get_barrier_semaphore()
+    for where in (beside, across, core):
+        pl.semaphore_signal(barrier, inc=1, device_id=where, device_id_type=MESH)
+
+    @pl.when(z > 0)
+    def _():
+        pl.semaphore_signal(barrier, inc=1, device_id=below, device_id_type=MESH)
+
+    @pl.when(z < PLANES - 1)
+    def _():
+        pl.semaphore_signal(barrier, inc=1, device_id=above, device_id_type=MESH)
+
+    fetch = pltpu.make_async_copy(codes_hbm, codes, codes_sem)
+    fetch.start()
+
+    def plane_of(k):
+        step_end = k
+        step_middle = (-1, 1, 2)[k - 1]
+        return z + sign * (step_end + middle * (step_middle - step_end))
+
+    def piece(plane, side, c):
+        start = pl.multiple_of((plane * 2 + side) * count + c * step, step)
+        return prepared.at[pl.ds(start, step), :]
+
+    def hop(plane, side, c, send_sem, where):
+        block = piece(plane, side, c)
+        return pltpu.make_async_remote_copy(
+            src_ref=block, dst_ref=block, send_sem=send_sem, recv_sem=recv_sem.at[plane * 2 + side, c],
+            device_id=where, device_id_type=MESH,
+        )
+
+    def up(plane, c):
+        return hop(plane, x, c, up_sem.at[plane, c], above)
+
+    def down(plane, c):
+        return hop(plane, x, c, down_sem.at[plane, c], below)
+
+    def over_x(plane, c):
+        return hop(plane, x, c, x_sem.at[plane, c], beside)
+
+    def over_y(plane, c):
+        return hop(plane, 1 - x, c, y_sem.at[plane, c], across)
+
+    def landed(plane, side, c):
+        hop(plane, side, c, up_sem.at[0, 0], beside).wait_recv()
+
+    for ref, diag in ((right_ref, right_diag), (left_ref, left_diag)):
+        tall = jnp.concatenate([ref[...]] * 4, axis=0)
+        wide = jnp.concatenate([jnp.concatenate([tall, tall], axis=1)] * 2, axis=1)
+        row_at = lax.broadcasted_iota(jnp.int32, wide.shape, 0) // order
+        col_at = lax.broadcasted_iota(jnp.int32, wide.shape, 1) // order
+        high, low = split(jnp.where(row_at == col_at, wide, 0.0))
+        diag[0] = high
+        diag[1] = low
+
+    lane = lax.broadcasted_iota(jnp.int32, (step, 128), 1)
+
+    def prepare(c):
+        piece_of = queries_ref[c * step : (c + 1) * step, :]
+        groups = width // 256
+        stacked = jnp.concatenate([piece_of[:, g * 256 : (g + 1) * 256] for g in range(groups)], axis=0)
+        result = dot(stacked, right_diag[0]) + dot(stacked, right_diag[1])
+        for pair in range(width // 128):
+            g, h = pair // 2, pair % 2
+            value = result[g * step : (g + 1) * step, h * 128 : (h + 1) * 128]
+            spread[pl.ds(2 * pair, step, stride=order), :] = value
+            spread[pl.ds(2 * pair + 1, step, stride=order), :] = pltpu.roll(value, 64, 1)
+        for i in range(step // 4):
+            high, low = split(spread[i * 256 : (i + 1) * 256, :])
+            mixed[i * 256 : (i + 1) * 256, :] = (
+                dot(left_diag[0], high) + dot(left_diag[1], high) + dot(left_diag[0], low)
+            )
+        start = pl.multiple_of(at * count + c * step, step)
+        for pair in range(width // 128):
+            even = mixed[pl.ds(2 * pair, step, stride=order), :]
+            odd = pltpu.roll(mixed[pl.ds(2 * pair + 1, step, stride=order), :], 64, 1)
+            prepared[pl.ds(start, step), pair * 128 : (pair + 1) * 128] = jnp.where(
+                lane < 64, even, odd
+            ).astype(jnp.bfloat16)
+
+    def spread_out(plane, c):
+        @pl.when(c % 2 == y)
+        def _():
+            over_x(plane, c).start()
+
+    def relay_y(plane, c):
+        @pl.when(c % 2 == y)
+        def _():
+            landed(plane, 1 - x, c)
+            over_y(plane, c).start()
+
+    def finish_y(plane):
+        for c in range(CHUNKS):
+            @pl.when(c % 2 != y)
+            def _():
+                landed(plane, 1 - x, c)
+
+    def exchange(plane):
+        return pltpu.make_async_remote_copy(
+            src_ref=mine.at[plane, 1 - layer], dst_ref=theirs.at[plane],
+            send_sem=part_sem.at[plane], recv_sem=part_recv_sem.at[plane],
+            device_id=core, device_id_type=MESH,
+        )
+
+    def score(plane):
+        start = pl.multiple_of(plane * 2 * count, 2 * count)
+        for h in range(2):
+            mine[plane, h] = lax.dot_general(
+                train[h * half : (h + 1) * half, :], prepared[pl.ds(start, 2 * count), :],
+                (((1,), (1,)), ((), ())), preferred_element_type=jnp.float32,
+            )
+        exchange(plane).start()
+
+    def dequantize():
+        @pl.loop(0, rows // 64)
+        def _(t):
+            span = pl.ds(pl.multiple_of(t * 64, 64), 64)
+            for j in range(width // 128):
+                train[span, j * 128 : (j + 1) * 128] = (
+                    codes[span, j * 128 : (j + 1) * 128].astype(jnp.float32) * scales[span, j : j + 1]
+                ).astype(jnp.bfloat16)
+
+    for c in range(CHUNKS):
+        prepare(c)
+        if c == 0:
+            pl.semaphore_wait(barrier, 3 + jnp.minimum(z, 1) + jnp.minimum(PLANES - 1 - z, 1))
+
+        @pl.when(z < PLANES - 1)
+        def _():
+            up(z, c).start()
+
+        @pl.when(z > 0)
+        def _():
+            down(z, c).start()
+
+        spread_out(z, c)
+
+    fetch.wait()
+    scales[...] = scales_ref[...].T
+    relay_y(z, 0)
+    relay_y(z, 1)
+    dequantize()
+    relay_y(z, 2)
+    relay_y(z, 3)
+
+    def event(e):
+        k_end, c_end = 1 + e // CHUNKS, e % CHUNKS
+        if e < 2 * CHUNKS:
+            k_mid, c_mid = 1 + e % 2, e // 2
+        else:
+            k_mid, c_mid = k_end, c_end
+        plane = plane_of(k_end) + middle * (plane_of(k_mid) - plane_of(k_end))
+        return plane, c_end + middle * (c_mid - c_end)
+
+    for e in range(EVENTS):
+        plane, c = event(e)
+        landed(plane, x, c)
+
+        @pl.when((plane < z) & (z < PLANES - 1))
+        def _():
+            up(plane, c).start()
+
+        @pl.when((plane > z) & (z > 0))
+        def _():
+            down(plane, c).start()
+
+        spread_out(plane, c)
+        if e >= 2:
+            relay_y(*event(e - 2))
+        if e == 3:
+            finish_y(z)
+            score(z)
+        if e == EVENTS - 2:
+            first = plane_of(1)
+            finish_y(first)
+            score(first)
+    relay_y(*event(EVENTS - 2))
+    relay_y(*event(EVENTS - 1))
+    for k in (2, 3):
+        plane = plane_of(k)
+        finish_y(plane)
+        score(plane)
+
+    for plane in [z] + [plane_of(k) for k in (1, 2, 3)]:
+        exchange(plane).wait()
+        start = pl.multiple_of(plane * 2 * count, 2 * count)
+        out_ref[:, pl.ds(start, 2 * count)] = mine[plane, layer] + theirs[plane]
+
+    for plane in range(PLANES):
+        for c in range(CHUNKS):
+            @pl.when((plane <= z) & (z < PLANES - 1))
+            def _():
+                up(plane, c).wait_send()
+
+            @pl.when((plane >= z) & (z > 0))
+            def _():
+                down(plane, c).wait_send()
+
+            @pl.when(c % 2 == y)
+            def _():
+                over_x(plane, c).wait_send()
+                over_y(plane, c).wait_send()
+
+
+def per_device_kernel(train_codes, block_scales, queries, left_factor, right_factor):
+    rows, _, width = train_codes.shape
+    count = queries.shape[0]
+    order = left_factor.shape[1]
+    step = count // CHUNKS
+    blocks = block_scales.shape[2]
+    total = 2 * PLANES * count
+    vmem = pl.BlockSpec(memory_space=pltpu.VMEM)
+    return pl.pallas_call(
+        score_kernel,
+        out_shape=jax.ShapeDtypeStruct((rows // 2, total), jnp.float32),
+        in_specs=[pl.BlockSpec(memory_space=pl.ANY)] + [vmem] * 4,
+        out_specs=vmem,
+        scratch_shapes=[
+            pltpu.VMEM((rows, width), jnp.bfloat16),
+            pltpu.VMEM((rows, width), jnp.bfloat16),
+            pltpu.VMEM((rows, blocks), jnp.float32),
+            pltpu.VMEM((total, width), jnp.bfloat16),
+            pltpu.VMEM((step * order, 128), jnp.float32),
+            pltpu.VMEM((step * order, 128), jnp.float32),
+            pltpu.VMEM((2, 4 * order, 4 * order), jnp.bfloat16),
+            pltpu.VMEM((2, 4 * order, 4 * order), jnp.bfloat16),
+            pltpu.VMEM((PLANES, 2, rows // 2, 2 * count), jnp.float32),
+            pltpu.VMEM((PLANES, rows // 2, 2 * count), jnp.float32),
+            pltpu.SemaphoreType.DMA,
+            pltpu.SemaphoreType.DMA((2 * PLANES, CHUNKS)),
+            pltpu.SemaphoreType.DMA((PLANES, CHUNKS)),
+            pltpu.SemaphoreType.DMA((PLANES, CHUNKS)),
+            pltpu.SemaphoreType.DMA((PLANES, CHUNKS)),
+            pltpu.SemaphoreType.DMA((PLANES, CHUNKS)),
+            pltpu.SemaphoreType.DMA((PLANES,)),
+            pltpu.SemaphoreType.DMA((PLANES,)),
+        ],
+        compiler_params=pltpu.CompilerParams(
+            collective_id=0, has_side_effects=True, vmem_limit_bytes=40 * 1024 * 1024
+        ),
+        cost_estimate=pl.CostEstimate(
+            flops=2 * rows * total * width, bytes_accessed=2 * rows * width, transcendentals=0
+        ),
+        name="score_kernel",
+    )(
+        train_codes.reshape(rows, width),
+        block_scales.reshape(rows, blocks).T,
+        queries.reshape(count, width),
+        left_factor[0],
+        right_factor[0],
+    )
 
 def precondition(flat, left_factor, right_factor):
     count = flat.shape[0]
@@ -36,8 +326,9 @@
 
 
 def solution(mesh):
+    small = mesh.shape["grp"] == 2 and mesh.shape["row"] == 2 * PLANES and mesh.shape["layer"] == 2
     return jax.shard_map(
-        per_device,
+        per_device_kernel if small else per_device,
         mesh=mesh,
         in_specs=(
             P(("grp", "row"), "layer", None),

time: 113 us -> 58.3 us (0.52)
  waiting for transfers between devices: 83 us -> 0 us
  Pallas kernels: 0 us -> 51.5 us
  between operations: 13.5 us -> 0.01 us
  matrix products: 8.84 us -> 0 us
    all_gather x1 -> x0, waiting for transfers between devices: 76.1 us -> none  [per_device(): lax.all_gather(sending, 'row', axis=0, tiled=True)]
    pallas_call x0 -> x1, Pallas kernels: none -> 51.5 us  [per_device_kernel(): pl.pallas_call(score_kernel, out_shape=jax.ShapeDtypeStruct((rows // 2, t...]
    dot_general x3 -> x0, matrix products: 8.84 us -> none  [the longest x1 6.09 us: per_device(): jnp.einsum('rk,qk->rq', dequant, lax.all_gather(sending, 'row', axis=0, t...]
    reduce_scatter x1 -> x0, waiting for transfers between devices: 6.95 us -> none  [per_device(): lax.psum_scatter(partial_scores, 'layer', scatter_dimension=0, tiled=True)]
    unnamed x10 -> x11, local copies, waits for them, and re-layouts: 1.17 us -> 6.38 us
    mul x2 -> x0, local copies, waits for them, and re-layouts: 2.41 us -> none  [per_device(): train_codes.reshape(rows, layers, blocks, width // blocks)]
    another operation x1 -> x0, local copies, waits for them, and re-layouts: 2.07 us -> none
    reshape x1 -> x0, local copies, waits for them, and re-layouts: 1.61 us -> none  [precondition(): return result.astype(jnp.bfloat16).reshape(count, layers * outer * inner)]
  transfers between devices with their start and end apart: 2 -> 0, of which waited for: 2 -> 0; matrix products, arithmetic and copies ran while one was open for 0% -> 0% of each run, Pallas kernels for 0% -> 0%
where the time goes in v1:
time: 58.3 us; the launch traced here: 57.9 us
  Pallas kernels  51.5 us (88%)
  local copies, waits for them, and re-layouts  6.38 us (11%)
    pallas_call x1, Pallas kernels, per_device_kernel(): pl.pallas_call(score_kernel, out_shape=jax.ShapeDtypeStruct((rows // 2, t...  51.5 us
    unnamed x11, local copies, waits for them, and re-layouts  6.38 us

profile of v1, /device:TPU:0, one launch (start us, length us, event | category | flops | bytes accessed | tf_op | source)
XLA Modules:
  0.0 57.9 jit_solution(10330279350883485900)
XLA Ops:
  0.0 0.0 copy-start
  0.0 2.2 %copy-done = bf16[512,1,4096]{2,0,1:T(8,128)(2,1)S(1)} copy-done((bf16[512,1,4096]{2,0,1:T(8,128)(2,1)S(1)}, bf16[512,1,4096]{2,0,1:T(8,128)(2,1)}, u32[]{:S(2)}) %copy-start) | copy-done | bytes 4194328
  2.2 0.0 copy-start.1
  2.2 1.0 %copy-done.1 = bf16[64,1,4096]{2,0,1:T(8,128)(2,1)S(1)} copy-done((bf16[64,1,4096]{2,0,1:T(8,128)(2,1)S(1)}, bf16[64,1,4096]{2,0,1:T(8,128)(2,1)}, u32[]{:S(2)}) %copy-start.1) | copy-done | bytes 524312
  3.2 0.0 copy-start.2
  3.2 0.8 %copy-done.2 = f32[512,1,32]{0,2,1:T(8,128)S(1)} copy-done((f32[512,1,32]{0,2,1:T(8,128)S(1)}, f32[512,1,32]{0,2,1:T(8,128)}, u32[]{:S(2)}) %copy-start.2) | copy-done | bytes 65560
  4.1 0.0 copy-start.3
  4.1 0.8 %copy-done.3 = f32[1,64,64]{2,1,0:T(8,128)S(1)} copy-done((f32[1,64,64]{2,1,0:T(8,128)S(1)}, f32[1,64,64]{2,1,0:T(8,128)}, u32[]{:S(2)}) %copy-start.3) | copy-done | bytes 16408
  4.8 0.0 copy-start.4
  4.8 0.8 %copy-done.4 = f32[1,64,64]{2,1,0:T(8,128)S(1)} copy-done((f32[1,64,64]{2,1,0:T(8,128)S(1)}, f32[1,64,64]{2,1,0:T(8,128)}, u32[]{:S(2)}) %copy-start.4) | copy-done | bytes 16408
  5.6 51.5 %score_kernel.1 = f32[256,512]{1,0:T(8,128)S(1)} custom-call(bf16[512,4096]{1,0:T(8,128)(2,1)S(1)} %bitcast.7, f32[32,512]{1,0:T(8,128)S(1)} %bitcast.9, bf16[64,4096]{1,0:T(8,128)(2,1)S(1)} %bitcast.8, f32[64,64]{1,0:T(8,128)S(1)} %bitcast.10, f32[64,64]{1,0:T(8,128)S(1)} %bitcast.11), custom_call_target="tpu_custom_call" | custom-call | flops 2147483648 | bytes 4194304 | tf_op jit(solution)/shard_map/score_kernel/pallas_call | solution.py:257
  57.1 0.8 %copy.7 = f32[256,512]{1,0:T(8,128)} copy(f32[256,512]{1,0:T(8,128)S(1)} %score_kernel.1) | data formatting | bytes 1048576
Async XLA Ops:
  0.0 2.2 %copy-start = (bf16[512,1,4096]{2,0,1:T(8,128)(2,1)S(1)}, bf16[512,1,4096]{2,0,1:T(8,128)(2,1)}, u32[]{:S(2)}) copy-start(bf16[512,1,4096]{2,0,1:T(8,128)(2,1)} %param.5) | copy-start | bytes 12582916
  2.2 1.0 %copy-start.1 = (bf16[64,1,4096]{2,0,1:T(8,128)(2,1)S(1)}, bf16[64,1,4096]{2,0,1:T(8,128)(2,1)}, u32[]{:S(2)}) copy-start(bf16[64,1,4096]{2,0,1:T(8,128)(2,1)} %param.7) | copy-start | bytes 1572868
  3.2 0.8 %copy-start.2 = (f32[512,1,32]{0,2,1:T(8,128)S(1)}, f32[512,1,32]{0,2,1:T(8,128)}, u32[]{:S(2)}) copy-start(f32[512,1,32]{0,2,1:T(8,128)} %param.6) | copy-start | bytes 196612
  4.1 0.8 %copy-start.3 = (f32[1,64,64]{2,1,0:T(8,128)S(1)}, f32[1,64,64]{2,1,0:T(8,128)}, u32[]{:S(2)}) copy-start(f32[1,64,64]{2,1,0:T(8,128)} %param.8) | copy-start | bytes 49156
  4.8 0.8 %copy-start.4 = (f32[1,64,64]{2,1,0:T(8,128)S(1)}, f32[1,64,64]{2,1,0:T(8,128)}, u32[]{:S(2)}) copy-start(f32[1,64,64]{2,1,0:T(8,128)} %param.9) | copy-start | bytes 49156

commit v2 on v1

v2 whole, which is shorter than its diff:
```python
import jax
import jax.numpy as jnp
from jax import lax
from jax.experimental import pallas as pl
from jax.experimental.pallas import tpu as pltpu
from jax.sharding import PartitionSpec as P

MESH = pl.DeviceIdType.MESH
PLANES = 4
GROUPS = 4
SINGLE = 2
LAG = 4
AHEAD = 4
CARRIED = [(g, other) for g in range(GROUPS) for other in range(2) if not (other and g < SINGLE)]


def split(value):
    high = value.astype(jnp.bfloat16)
    return high, (value - high.astype(jnp.float32)).astype(jnp.bfloat16)


def dot(a, b):
    return jnp.dot(a, b, preferred_element_type=jnp.float32)


def score_kernel(
    codes_hbm, scales_hbm, queries_hbm, left_hbm, right_hbm, out_hbm,
    codes, train, flat_scales, scales, queries, left, right, prepared, spread, mixed,
    left_diag, right_diag, mine, theirs, result,
    fetch_sem, query_sem, out_sem, recv_sem, up_sem, down_sem, x_sem, relay_sem, y_sem, part_sem, part_recv_sem,
):
    rows, width = codes.shape
    order = left.shape[0]
    count = queries.shape[0]
    step = count // GROUPS
    half = rows // 2
    y, at, layer = lax.axis_index("grp"), lax.axis_index("row"), lax.axis_index("layer")
    z, x = at // 2, at % 2
    middle = (z * (PLANES - 1 - z)) // 2
    sign = 1 - 2 * (z // 2)
    above = {"row": at + 2}
    below = {"row": at - 2}
    beside = {"row": at + 1 - 2 * x}
    across = {"grp": 1 - y}
    core = {"layer": 1 - layer}

    barrier = pltpu.get_barrier_semaphore()
    for where in (beside, across, core):
        pl.semaphore_signal(barrier, inc=1, device_id=where, device_id_type=MESH)

    @pl.when(z > 0)
    def _():
        pl.semaphore_signal(barrier, inc=1, device_id=below, device_id_type=MESH)

    @pl.when(z < PLANES - 1)
    def _():
        pl.semaphore_signal(barrier, inc=1, device_id=above, device_id_type=MESH)

    def fetch_queries(g):
        span = pl.ds(g * step, step)
        return pltpu.make_async_copy(queries_hbm.at[span, :], queries.at[span, :], query_sem.at[g])

    fetch_left = pltpu.make_async_copy(left_hbm, left, fetch_sem.at[0])
    fetch_right = pltpu.make_async_copy(right_hbm, right, fetch_sem.at[1])
    fetch_scales = pltpu.make_async_copy(scales_hbm, flat_scales, fetch_sem.at[2])
    fetch_codes = pltpu.make_async_copy(codes_hbm, codes, fetch_sem.at[3])
    fetch_right.start()
    fetch_left.start()
    for g in range(GROUPS):
        fetch_queries(g).start()
    fetch_scales.start()
    fetch_codes.start()

    def plane_of(k):
        step_middle = (1, -1, 2)[k - 1]
        return z + sign * (k + middle * (step_middle - k))

    def half_of(other):
        return y + other * (1 - 2 * y)

    def piece(plane, side, g, h):
        start = pl.multiple_of((plane * 2 + side) * count + g * step, step)
        return prepared.at[pl.ds(start, step), pl.ds(pl.multiple_of(h * (width // 2), width // 2), width // 2)]

    def hop(plane, side, g, other, send_sem, where):
        h = half_of(other)
        block = piece(plane, side, g, h)
        return pltpu.make_async_remote_copy(
            src_ref=block, dst_ref=block, send_sem=send_sem, recv_sem=recv_sem.at[plane * 2 + side, 2 * g + h],
            device_id=where, device_id_type=MESH,
        )

    def up(plane, g, other):
        return hop(plane, x, g, other, up_sem.at[plane, 2 * g + other], above)

    def down(plane, g, other):
        return hop(plane, x, g, other, down_sem.at[plane, 2 * g + other], below)

    def over_x(plane, g, other):
        return hop(plane, x, g, other, x_sem.at[plane, 2 * g + other], beside)

    def over_y(plane, g):
        return hop(plane, x, g, 0, y_sem.at[plane, g], across)

    def relayed(plane, g):
        return hop(plane, 1 - x, g, 0, relay_sem.at[plane, g], across)

    def landed(plane, side, g, other):
        hop(plane, side, g, other, up_sem.at[0, 0], beside).wait_recv()

    def fill_diag(ref, diag):
        tall = jnp.concatenate([ref[...]] * 4, axis=0)
        wide = jnp.concatenate([jnp.concatenate([tall, tall], axis=1)] * 2, axis=1)
        row_at = lax.broadcasted_iota(jnp.int32, wide.shape, 0) // order
        col_at = lax.broadcasted_iota(jnp.int32, wide.shape, 1) // order
        high, low = split(jnp.where(row_at == col_at, wide, 0.0))
        diag[0] = high
        diag[1] = low

    lane = lax.broadcasted_iota(jnp.int32, (step, 128), 1)

    def prepare(c):
        fetch_queries(c).wait()
        piece_of = queries[c * step : (c + 1) * step, :]
        stacked = jnp.concatenate([piece_of[:, g * 256 : (g + 1) * 256] for g in range(width // 256)], axis=0)
        turned = dot(stacked, right_diag[0]) + dot(stacked, right_diag[1])
        for pair in range(width // 128):
            g, h = pair // 2, pair % 2
            value = turned[g * step : (g + 1) * step, h * 128 : (h + 1) * 128]
            spread[pl.ds(2 * pair, step, stride=order), :] = value
            spread[pl.ds(2 * pair + 1, step, stride=order), :] = pltpu.roll(value, 64, 1)
        for i in range(step // 4):
            high, low = split(spread[i * 256 : (i + 1) * 256, :])
            mixed[i * 256 : (i + 1) * 256, :] = (
                dot(left_diag[0], high) + dot(left_diag[1], high) + dot(left_diag[0], low)
            )
        start = pl.multiple_of(at * count + c * step, step)
        for pair in range(width // 128):
            even = mixed[pl.ds(2 * pair, step, stride=order), :]
            odd = pltpu.roll(mixed[pl.ds(2 * pair + 1, step, stride=order), :], 64, 1)
            prepared[pl.ds(start, step), pair * 128 : (pair + 1) * 128] = jnp.where(
                lane < 64, even, odd
            ).astype(jnp.bfloat16)

    def relay(plane, g):
        landed(plane, 1 - x, g, 0)
        relayed(plane, g).start()

    def finish_own():
        landed(z, 1 - x, 0, 1)
        for g in range(1, GROUPS):
            landed(z, 1 - x, g, 0)
            landed(z, 1 - x, g, 1)

    def finish(plane):
        for g in range(GROUPS):
            if g < SINGLE:
                landed(plane, x, g, 1)
            landed(plane, 1 - x, g, 1)

    def exchange(plane):
        return pltpu.make_async_remote_copy(
            src_ref=mine.at[plane, 1 - layer], dst_ref=theirs.at[plane],
            send_sem=part_sem.at[plane], recv_sem=part_recv_sem.at[plane],
            device_id=core, device_id_type=MESH,
        )

    def score(plane):
        start = pl.multiple_of(plane * 2 * count, 2 * count)
        for h in range(2):
            mine[plane, h] = lax.dot_general(
                train[h * half : (h + 1) * half, :], prepared[pl.ds(start, 2 * count), :],
                (((1,), (1,)), ((), ())), preferred_element_type=jnp.float32,
            )
        exchange(plane).start()

    def give(plane):
        start = pl.multiple_of(plane * 2 * count, 2 * count)
        return pltpu.make_async_copy(result.at[plane], out_hbm.at[:, pl.ds(start, 2 * count)], out_sem.at[plane])

    def combine(plane):
        exchange(plane).wait()
        result[plane] = mine[plane, layer] + theirs[plane]
        give(plane).start()

    def dequantize(part):
        @pl.loop(0, rows // (64 * GROUPS))
        def _(t):
            span = pl.ds(pl.multiple_of(part * (rows // GROUPS) + t * 64, 64), 64)
            for j in range(width // 128):
                train[span, j * 128 : (j + 1) * 128] = (
                    codes[span, j * 128 : (j + 1) * 128].astype(jnp.float32) * scales[span, j : j + 1]
                ).astype(jnp.bfloat16)

    fetch_right.wait()
    fill_diag(right, right_diag)
    fetch_left.wait()
    fill_diag(left, left_diag)
    def send_own(g, other):
        @pl.when(z < PLANES - 1)
        def _():
            up(z, g, other).start()

        @pl.when(z > 0)
        def _():
            down(z, g, other).start()

    def outward(plane, g, other):
        @pl.when(z == 1)
        def _():
            down(plane, g, other).start()

        @pl.when(z == 2)
        def _():
            up(plane, g, other).start()

    def inward(plane, g, other):
        @pl.when(z == 1)
        def _():
            up(plane, g, other).start()

        @pl.when(z == 2)
        def _():
            down(plane, g, other).start()

    later = []
    for g in range(GROUPS):
        prepare(g)
        if g == 0:
            pl.semaphore_wait(barrier, 3 + jnp.minimum(z, 1) + jnp.minimum(PLANES - 1 - z, 1))
        for row_group, other in CARRIED[:AHEAD]:
            if row_group == g:
                send_own(g, other)
        if g == 0:
            over_x(z, 0, 0).start()
        elif g == 1:
            over_x(z, 1, 0).start()
            over_x(z, 1, 1).start()
        else:
            later += [(g, 0), (g, 1)]

    fetch_scales.wait()
    scales[...] = flat_scales[...].T
    fetch_codes.wait()
    relay(z, 0)

    events = [(k, g, other) for k in (1, 2, 3) for g, other in CARRIED]
    relays = {}
    for e, (k, g, other) in enumerate(events):
        if not other:
            relays.setdefault(e + LAG, []).append((k, g))
    for e, (k, g, other) in enumerate(events):
        plane = plane_of(k)
        if k == 1:
            landed(plane, x, g, other)
        else:
            @pl.when(middle == 0)
            def _():
                landed(plane, x, g, other)

        due = e + AHEAD
        each = len(CARRIED)
        if due < each:
            send_own(*CARRIED[due])
        elif due < 2 * each:
            due_piece = CARRIED[due - each]

            @pl.when(middle == 1)
            def _():
                outward(plane_of(1), *due_piece)
                landed(plane_of(2), x, *due_piece)
                inward(plane_of(2), *due_piece)
        elif due < 3 * each:
            due_piece = CARRIED[due - 2 * each]

            @pl.when(middle == 1)
            def _():
                landed(plane_of(3), x, *due_piece)
                outward(plane_of(3), *due_piece)

        if other:
            if later:
                over_x(z, *later.pop(0)).start()
        else:
            over_x(plane, g, 0).start()
            if g < SINGLE:
                over_y(plane, g).start()
        for late_k, late_g in relays.pop(e, []):
            relay(plane_of(late_k), late_g)
        if e in (1, 3, 5, 7):
            dequantize(e // 2)
        if e == 13:
            finish_own()
            score(z)
        if e == 15:
            finish(plane_of(1))
            score(plane_of(1))
    for e in sorted(relays):
        for late_k, late_g in relays[e]:
            relay(plane_of(late_k), late_g)
    finish(plane_of(2))
    score(plane_of(2))
    combine(z)
    combine(plane_of(1))
    finish(plane_of(3))
    score(plane_of(3))
    combine(plane_of(2))
    combine(plane_of(3))

    for plane in range(PLANES):
        for g, other in CARRIED:
            @pl.when((plane <= z) & (z < PLANES - 1))
            def _():
                up(plane, g, other).wait_send()

            @pl.when((plane >= z) & (z > 0))
            def _():
                down(plane, g, other).wait_send()

    over_x(z, 0, 0).wait_send()
    relayed(z, 0).wait_send()
    for g in range(1, GROUPS):
        over_x(z, g, 0).wait_send()
        over_x(z, g, 1).wait_send()
    for k in (1, 2, 3):
        for g in range(GROUPS):
            over_x(plane_of(k), g, 0).wait_send()
            relayed(plane_of(k), g).wait_send()
            if g < SINGLE:
                over_y(plane_of(k), g).wait_send()
    for plane in range(PLANES):
        give(plane).wait()


def per_device_kernel(train_codes, block_scales, queries, left_factor, right_factor):
    rows, _, width = train_codes.shape
    count = queries.shape[0]
    order = left_factor.shape[1]
    step = count // GROUPS
    blocks = block_scales.shape[2]
    total = 2 * PLANES * count
    hbm = pl.BlockSpec(memory_space=pl.ANY)
    return pl.pallas_call(
        score_kernel,
        out_shape=jax.ShapeDtypeStruct((rows // 2, total), jnp.float32),
        in_specs=[hbm] * 5,
        out_specs=hbm,
        scratch_shapes=[
            pltpu.VMEM((rows, width), jnp.bfloat16),
            pltpu.VMEM((rows, width), jnp.bfloat16),
            pltpu.VMEM((blocks, rows), jnp.float32),
            pltpu.VMEM((rows, blocks), jnp.float32),
            pltpu.VMEM((count, width), jnp.bfloat16),
            pltpu.VMEM((order, order), jnp.float32),
            pltpu.VMEM((order, order), jnp.float32),
            pltpu.VMEM((total, width), jnp.bfloat16),
            pltpu.VMEM((step * order, 128), jnp.float32),
            pltpu.VMEM((step * order, 128), jnp.float32),
            pltpu.VMEM((2, 4 * order, 4 * order), jnp.bfloat16),
            pltpu.VMEM((2, 4 * order, 4 * order), jnp.bfloat16),
            pltpu.VMEM((PLANES, 2, rows // 2, 2 * count), jnp.float32),
            pltpu.VMEM((PLANES, rows // 2, 2 * count), jnp.float32),
            pltpu.VMEM((PLANES, rows // 2, 2 * count), jnp.float32),
            pltpu.SemaphoreType.DMA((4,)),
            pltpu.SemaphoreType.DMA((GROUPS,)),
            pltpu.SemaphoreType.DMA((PLANES,)),
            pltpu.SemaphoreType.DMA((2 * PLANES, 2 * GROUPS)),
            pltpu.SemaphoreType.DMA((PLANES, 2 * GROUPS)),
            pltpu.SemaphoreType.DMA((PLANES, 2 * GROUPS)),
            pltpu.SemaphoreType.DMA((PLANES, 2 * GROUPS)),
            pltpu.SemaphoreType.DMA((PLANES, GROUPS)),
            pltpu.SemaphoreType.DMA((PLANES, GROUPS)),
            pltpu.SemaphoreType.DMA((PLANES,)),
            pltpu.SemaphoreType.DMA((PLANES,)),
        ],
        compiler_params=pltpu.CompilerParams(
            collective_id=0, has_side_effects=True, vmem_limit_bytes=60 * 1024 * 1024
        ),
        cost_estimate=pl.CostEstimate(
            flops=2 * rows * total * width, bytes_accessed=2 * rows * width, transcendentals=0
        ),
        name="score_kernel",
    )(
        train_codes.reshape(rows, width),
        block_scales.reshape(rows, blocks).T,
        queries.reshape(count, width),
        left_factor.reshape(order, order),
        right_factor.reshape(order, order),
    )


def precondition(flat, left_factor, right_factor):
    count = flat.shape[0]
    layers = left_factor.shape[0]
    outer = left_factor.shape[1]
    inner = right_factor.shape[1]
    blocks = flat.reshape(count, layers, outer, inner).astype(jnp.float32)
    result = jnp.einsum(
        "lab,nlbc,lcd->nlad", left_factor, blocks, right_factor, precision=lax.Precision.HIGHEST
    )
    return result.astype(jnp.bfloat16).reshape(count, layers * outer * inner)


def per_device(train_codes, block_scales, queries, left_factor, right_factor):
    rows, layers, width = train_codes.shape
    blocks = block_scales.shape[2]
    values = (
        train_codes.reshape(rows, layers, blocks, width // blocks).astype(jnp.float32)
        * block_scales[..., None]
    )
    dequant = values.astype(jnp.bfloat16).reshape(rows, layers * width)
    flat = queries.reshape(queries.shape[0], layers * width)
    sending = precondition(flat, left_factor, right_factor)
    partial_scores = jnp.einsum(
        "rk,qk->rq",
        dequant,
        lax.all_gather(sending, "row", axis=0, tiled=True),
        preferred_element_type=jnp.float32,
    )
    return lax.psum_scatter(partial_scores, "layer", scatter_dimension=0, tiled=True)


def solution(mesh):
    small = mesh.shape["grp"] == 2 and mesh.shape["row"] == 2 * PLANES and mesh.shape["layer"] == 2
    return jax.shard_map(
        per_device_kernel if small else per_device,
        mesh=mesh,
        in_specs=(
            P(("grp", "row"), "layer", None),
            P(("grp", "row"), "layer", None),
            P("row", "layer", None),
            P("layer", None, None),
            P("layer", None, None),
        ),
        out_specs=P(("grp", "row", "layer"), None),
        check_vma=False,
    )
```

time: 58.3 us -> 45.3 us (0.78)
  Pallas kernels: 51.5 us -> 43.3 us
  local copies, waits for them, and re-layouts: 6.38 us -> 1.87 us
    pallas_call x1, Pallas kernels: 51.5 us -> 43.3 us  [per_device_kernel(): pl.pallas_call(score_kernel, out_shape=jax.ShapeDtypeStruct((rows // 2, t...]
    unnamed x11 -> x1, local copies, waits for them, and re-layouts: 6.38 us -> 1.87 us
where the time goes in v2:
time: 45.3 us; the launch traced here: 45.1 us
  Pallas kernels  43.3 us (96%)
  local copies, waits for them, and re-layouts  1.87 us (4%)
    pallas_call x1, Pallas kernels, per_device_kernel(): pl.pallas_call(score_kernel, out_shape=jax.ShapeDtypeStruct((rows // 2, t...  43.3 us
    unnamed x1, local copies, waits for them, and re-layouts  1.87 us

profile of v2, /device:TPU:0, one launch (start us, length us, event | category | flops | bytes accessed | tf_op | source)
XLA Modules:
  0.0 45.1 jit_solution(3391285787729048517)
XLA Ops:
  0.0 43.3 %score_kernel.1 = f32[256,512]{1,0:T(8,128)} custom-call(bf16[512,4096]{1,0:T(8,128)(2,1)} %bitcast.7, f32[32,512]{1,0:T(8,128)} %bitcast.9, bf16[64,4096]{1,0:T(8,128)(2,1)} %bitcast.8, f32[64,64]{1,0:T(8,128)} %bitcast.10, f32[64,64]{1,0:T(8,128)} %bitcast.11), custom_call_target="tpu_custom_call" | custom-call | flops 2147483648 | bytes 4194304 | tf_op jit(solution)/shard_map/score_kernel/pallas_call | solution.py:343
  43.3 1.9 %copy.7 = f32[256,512]{1,0:T(8,128)} copy(f32[256,512]{1,0:T(8,128)} %score_kernel.1) | data formatting | bytes 1048576

commit v3 on v2

--- a/solution.py
+++ b/solution.py
@@ -9,9 +9,9 @@
 PLANES = 4
 GROUPS = 4
 SINGLE = 2
-LAG = 4
+LAG = 3
 AHEAD = 4
-CARRIED = [(g, other) for g in range(GROUPS) for other in range(2) if not (other and g < SINGLE)]
+CARRIED = [(g, other) for other in range(2) for g in range(GROUPS) if not (other and g < SINGLE)]
 
 
 def split(value):

time: 45.3 us -> 44.2 us (0.976)
  Pallas kernels: 43.3 us -> 42.2 us
    pallas_call x1, Pallas kernels: 43.3 us -> 42.2 us  [per_device_kernel(): pl.pallas_call(score_kernel, out_shape=jax.ShapeDtypeStruct((rows // 2, t...]
where the time goes in v3:
time: 44.2 us; the launch traced here: 44 us
  Pallas kernels  42.2 us (95%)
  local copies, waits for them, and re-layouts  1.87 us (4%)
    pallas_call x1, Pallas kernels, per_device_kernel(): pl.pallas_call(score_kernel, out_shape=jax.ShapeDtypeStruct((rows // 2, t...  42.2 us
    unnamed x1, local copies, waits for them, and re-layouts  1.87 us

profile of v3, /device:TPU:0, one launch (start us, length us, event | category | flops | bytes accessed | tf_op | source)
XLA Modules:
  0.0 44.0 jit_solution(6270832023604554285)
XLA Ops:
  0.0 42.2 %score_kernel.1 = f32[256,512]{1,0:T(8,128)} custom-call(bf16[512,4096]{1,0:T(8,128)(2,1)} %bitcast.7, f32[32,512]{1,0:T(8,128)} %bitcast.9, bf16[64,4096]{1,0:T(8,128)(2,1)} %bitcast.8, f32[64,64]{1,0:T(8,128)} %bitcast.10, f32[64,64]{1,0:T(8,128)} %bitcast.11), custom_call_target="tpu_custom_call" | custom-call | flops 2147483648 | bytes 4194304 | tf_op jit(solution)/shard_map/score_kernel/pallas_call | solution.py:343
  42.2 1.9 %copy.7 = f32[256,512]{1,0:T(8,128)} copy(f32[256,512]{1,0:T(8,128)} %score_kernel.1) | data formatting | bytes 1048576
